TPU v7x, 256 devices: a whole 4x4x8 slice. The times are simulated.
256 devices in a mesh: ctx: 64 (over z, y, core), kv: 4 (over x).
Axes of the slice: x: 4, y: 4, z: 8, core: 2. Of those that a mesh axis runs over, the one named last changes fastest.
Arguments:
- query: bfloat16 [2, 8192, 8192], P(None, 'ctx', 'kv')
- kv_rows: bfloat16 [2, 8192, 2048], P(None, 'ctx', 'kv')
- keep: int32 [2, 64, 8, 512], P(None, 'ctx', 'kv'), may hold values from 0 to 639, as said below
- dest: int32 [65536, 1], P('ctx'), may hold values from 0 to 255; in each aligned block of 1024 rows (0 to 1023, 1024 to 2047, ...) at most 8 rows name the same one
- offsets: int32 [2], replicated, may hold values from 0 to 62, as said below
Outputs:
- attention: bfloat16 [2, 8192, 8192], P(None, 'ctx', 'kv')
- row_scores: float32 [2, 8, 40960], P(None, 'kv', 'ctx')
- owner_cache: bfloat16 [131072, 2048], P(('ctx', 'kv'))
Inputs may be any that keep to these rules, and one draw needn't show every extreme that they name: `keep`: each list holds 512 distinct indices in increasing order; an index below 512 names a cache slot, an index k of 512 or more names span row k - 512. `dest`: among the 1024 rows of one context shard no owner is named more than 8 times; owner o is the device at position o in the ctx-major order of ctx and kv. `offsets`: one prompt starts at the first shard and another prompt at the second-to-last shard.
All inputs are finite; a program needn't handle non-finite values.
Results may differ from a plain program's by a relative error of at most 0.0049.
Values may be sent and summed in bfloat16 or wider, within the bound.
A program may use at most 192 MiB of HBM per device.

v0:
```python
import math
import jax
import jax.numpy as jnp
from jax import lax
from jax.sharding import PartitionSpec as P

HEAD = 128


def carried_in(value, axis, join, neutral):
    count, mine = (lax.axis_size(axis), lax.axis_index(axis))
    pieces = jax.tree.map(lambda part: lax.all_gather(part, axis), value)
    subtotal = jax.tree.map(
        lambda part, zero: jnp.full_like(part, 0) + jnp.asarray(zero, part.dtype), value, neutral
    )

    def hop(position, subtotal):
        longer = join(subtotal, jax.tree.map(lambda part: part[position], pieces))
        return jax.tree.map(lambda new, old: jnp.where(position < mine, new, old), longer, subtotal)

    return lax.fori_loop(0, count - 1, hop, subtotal)


def compose(earlier, later):
    early_marks, early_rows = earlier
    late_marks, late_rows = later
    length = late_marks.shape[-1]
    table = late_marks[..., None] == jnp.arange(length, dtype=jnp.int32)
    picked_marks = jnp.sum(jnp.where(table, early_marks[..., None, :], 0), axis=-1)
    marks = jnp.where(late_marks < length, picked_marks, late_marks)
    moved = jnp.einsum(
        "phst,pthc->pshc",
        table.astype(jnp.bfloat16),
        early_rows,
        preferred_element_type=jnp.float32,
    ).astype(jnp.bfloat16)
    carried = jnp.transpose(late_marks < length, (0, 2, 1))[..., None]
    rows = jnp.where(carried, moved, late_rows)
    return (marks.astype(jnp.int32), rows)


def local(query, kv_rows, keep, dest, offsets):
    prompts, span, qwidth = query.shape
    width = 2 * HEAD
    heads_dev = kv_rows.shape[2] // width
    cache_len = keep.shape[3]
    group = qwidth // (HEAD * heads_dev)
    position = lax.axis_index("ctx")
    active = position >= offsets
    keep_local = keep[:, 0]
    span_kv = kv_rows.reshape(prompts, span, heads_dev, width)
    slots = jnp.broadcast_to(
        jnp.arange(cache_len, dtype=jnp.int32), (prompts, heads_dev, cache_len)
    )
    own_marks = jnp.where(keep_local < cache_len, keep_local, cache_len)
    own_marks = jnp.where(active[:, None, None], own_marks, slots)
    picker = (keep_local[..., None] - cache_len == jnp.arange(span, dtype=jnp.int32)).astype(
        jnp.bfloat16
    )
    own_rows = jnp.einsum(
        "phst,pthc->pshc", picker, span_kv, preferred_element_type=jnp.float32
    ).astype(jnp.bfloat16)
    own_rows = jnp.where(active[:, None, None, None], own_rows, jnp.zeros_like(own_rows))
    identity = (slots, jnp.zeros_like(own_rows))
    incoming = carried_in((own_marks, own_rows), "ctx", compose, identity)
    in_marks, in_rows = incoming
    outgoing = compose(incoming, (own_marks, own_rows))
    rows_all = jnp.concatenate([in_rows, span_kv], axis=1)
    valid = in_marks >= cache_len
    qfive = query.reshape(prompts, span, heads_dev, group, HEAD)
    causal = jnp.arange(span)[None, :] <= jnp.arange(span)[:, None]
    scale = 1.0 / math.sqrt(HEAD)
    outputs = []
    masses = []
    for prompt in range(prompts):
        flag = active[prompt].astype(jnp.float32)
        head_outs = []
        head_mass = []
        for head in range(heads_dev):
            keys = rows_all[prompt, :, head, :HEAD]
            values = rows_all[prompt, :, head, HEAD:]
            attention_scores = (
                jnp.einsum(
                    "qgd,kd->gqk", qfive[prompt, :, head], keys, preferred_element_type=jnp.float32
                )
                * scale
            )
            seen = jnp.broadcast_to(valid[prompt, head][None, :], (span, cache_len))
            allowed = jnp.concatenate([seen, causal], axis=1)[None]
            attention_scores = jnp.where(allowed, attention_scores, -1e30)
            peak = jnp.max(attention_scores, axis=-1, keepdims=True)
            expo = jnp.where(allowed, jnp.exp(attention_scores - peak), 0.0)
            weights = expo / jnp.sum(expo, axis=-1, keepdims=True)
            mixed = jnp.einsum(
                "gqk,kd->qgd",
                weights.astype(jnp.bfloat16),
                values,
                preferred_element_type=jnp.float32,
            )
            head_outs.append((mixed * flag).astype(jnp.bfloat16))
            head_mass.append(jnp.sum(weights, axis=(0, 1)) * flag)
        outputs.append(jnp.stack(head_outs, axis=1))
        masses.append(jnp.stack(head_mass, axis=0))
    attention = jnp.stack(outputs, axis=0).reshape(prompts, span, qwidth)
    row_scores = jnp.stack(masses, axis=0)
    owner_count = lax.axis_size("ctx") * lax.axis_size("kv")
    capacity = 2 * prompts * cache_len // owner_count
    sending = outgoing[1].reshape(prompts * cache_len, heads_dev * width)
    owner_ids = dest[:, 0]
    onehot = (owner_ids[:, None] == jnp.arange(owner_count, dtype=jnp.int32)).astype(jnp.int32)
    rank = jnp.sum((jnp.cumsum(onehot, axis=0) - 1) * onehot, axis=1)
    target = owner_ids * capacity + rank
    placing = (
        target[None, :] == jnp.arange(owner_count * capacity, dtype=jnp.int32)[:, None]
    ).astype(jnp.bfloat16)
    packed = jnp.dot(placing, sending, preferred_element_type=jnp.float32).astype(jnp.bfloat16)
    packed = packed.reshape(lax.axis_size("ctx"), lax.axis_size("kv"), capacity, heads_dev * width)
    arrived = lax.all_to_all(
        lax.all_to_all(packed, "ctx", split_axis=0, concat_axis=0, tiled=True),
        "kv",
        split_axis=1,
        concat_axis=3,
        tiled=True,
    )
    owner_cache = arrived.reshape(-1, arrived.shape[3])
    return (attention, row_scores, owner_cache)


def solution(mesh):
    placed = (
        P(None, "ctx", "kv"),
        P(None, "ctx", "kv"),
        P(None, "ctx", "kv", None),
        P("ctx", None),
        P(),
    )
    return jax.shard_map(
        local,
        mesh=mesh,
        in_specs=placed,
        out_specs=(P(None, "ctx", "kv"), P(None, "kv", "ctx"), P(("ctx", "kv"), None)),
        check_vma=False,
    )
```

profile of v0, /device:TPU:32, one launch (start us, length us, event | category | flops | bytes accessed | tf_op | source)
XLA Modules:
  0.0 566.9 jit_solution(11673814230573235167)
XLA Ops:
  15.5 52.7 %all_gather.10 = s32[64,2,2,512]{3,2,1,0:T(2,128)S(1)} all-gather(s32[1,2,2,512]{3,2,1,0:T(2,128)S(1)} %fusion.131), channel_id=1, replica_groups=mesh['ctx'=64,'kv'=4] {'ctx'}, dimensions={0}, use_global_device_ids=true | all-gather | bytes 532480 | tf_op jit(solution)/shard_map/all_gather | solution.py:12
  68.7 181.0 %all-gather.3.cloned.1.call-done = bf16[128,512,2,256]{3,1,2,0:T(8,128)(2,1)} async-done(((bf16[2,512,2,256]{3,1,2,0:T(8,128)(2,1)}), bf16[128,512,2,256]{3,1,2,0:T(8,128)(2,1)}) %all-gather.3.cloned.1.call-update) | async-done | bytes 67108880 | tf_op jit(solution)/shard_map/all_gather | solution.py:12
  249.7 208.5 %while.16 = (s32[]{:T(128)}, s32[2,2,512]{2,1,0:T(2,128)S(1)}, bf16[2,512,2,256]{3,1,2,0:T(8,128)(2,1)S(1)}, s32[]{:T(128)}, s32[64,2,2,512]{3,2,1,0:T(2,128)S(1...) while((s32[]{:T(128)}, s32[2,2,512]{2,1,0:T(2,128)S(1)}, ...), condition=%wide.region_2.3_spmd.clone, body=%wide.region_0.2_spmd.clone.sunk | while | flops 543692800 | bytes 6381168 | solution.py:21
  249.8 2.3 fusion.176
  253.1 2.2 fusion.176
  256.5 2.2 fusion.176
  259.8 2.2 fusion.176
  263.1 2.2 fusion.176
  266.4 2.2 fusion.176
  269.7 2.2 fusion.176
  329.3 2.2 fusion.176
  392.1 2.2 fusion.176
  455.0 2.2 fusion.176
  460.8 3.7 fusion.18
  464.5 8.3 %all-to-all-start = ((bf16[64,4,8,512]{3,2,1,0:T(8,128)(2,1)}), bf16[64,4,8,512]{3,2,1,0:T(8,128)(2,1)S(1)}, u32[]{:S(2)}, u32[]{:S(2)}) async-start(bf16[64,4,8,512]{3,2,1,0:T(8,128)(2,1)} %bitcast.213), calls=%async_computation | async-start | bytes 4194304 | tf_op jit(solution)/shard_map/all_to_all | solution.py:119
  474.2 3.7 fusion.163
  477.9 3.6 fusion.160
  484.3 3.6 fusion.157
  487.9 3.6 fusion.156
  497.8 25.4 %all-to-all-done = bf16[64,4,8,512]{3,2,1,0:T(8,128)(2,1)S(1)} async-done(((bf16[64,4,8,512]{3,2,1,0:T(8,128)(2,1)}), bf16[64,4,8,512]{3,2,1,0:T(8,128)(2,1)S(1)}, u32[]{:S(2)}, u32[]{:S(2)}) %all-to-all-start) | async-done | bytes 2097184 | tf_op jit(solution)/shard_map/all_to_all | solution.py:119
  524.7 4.2 all-to-all-start.1
  532.9 2.3 fusion.79
  538.8 16.5 %all-to-all-done.1 = bf16[64,4,8,512]{3,2,0,1:T(8,128)(2,1)S(1)} async-done(((bf16[64,4,8,512]{3,2,0,1:T(8,128)(2,1)}), bf16[64,4,8,512]{3,2,0,1:T(8,128)(2,1)S(1)}, u32[]{:S(2)}, u32[]{:S(2)}) %all-to-all-start.1) | async-done | bytes 2097184 | tf_op jit(solution)/shard_map/all_to_all | solution.py:118
  555.4 2.7 copy.140
  (379 shorter events, 214.2 us)
Async XLA Ops:
  7.2 4.3 copy-start.5
  7.2 242.5 %all-gather.3.cloned.1.call-start = ((), (), s32[]{:S(2)}) async-start(), calls=%async_computation.2 | async-start | bytes 68157440 | tf_op jit(solution)/shard_map/all_gather | solution.py:12
  9.8 4.8 copy-start.8
  14.7 0.7 copy-start.7
  249.7 208.7 %copy-start.6 = (bf16[2,512,2,256]{3,1,2,0:T(8,128)(2,1)S(1)}, bf16[2,512,2,256]{3,1,2,0:T(8,128)(2,1)}, u32[]{:S(2)}) copy-start(bf16[2,512,2,256]{3,1,2,0:T(8,128)(2,1)} %fusion.26) | copy-start | bytes 3145732
  464.5 58.7 %all-to-all-start = ((bf16[64,4,8,512]{3,2,1,0:T(8,128)(2,1)}), bf16[64,4,8,512]{3,2,1,0:T(8,128)(2,1)S(1)}, u32[]{:S(2)}, u32[]{:S(2)}) async-start(bf16[64,4,8,512]{3,2,1,0:T(8,128)(2,1)} %bitcast.213), calls=%async_computation | async-start | bytes 4194304 | tf_op jit(solution)/shard_map/all_to_all | solution.py:119
  481.5 2.5 copy-start.3
  491.5 2.5 copy-start
  491.5 3.3 copy-start.2
  494.8 1.8 copy-start.4
  524.7 30.7 %all-to-all-start.1 = ((bf16[64,4,8,512]{3,2,0,1:T(8,128)(2,1)}), bf16[64,4,8,512]{3,2,0,1:T(8,128)(2,1)S(1)}, u32[]{:S(2)}, u32[]{:S(2)}) async-start(bf16[64,4,8,512]{3,2,0,1:T(8,128)(2,1)} %copy.116), calls=%async_computation.1 | async-start | bytes 4194304 | tf_op jit(solution)/shard_map/all_to_all | solution.py:118
  532.9 2.5 copy-start.1
Sparse Core Ops, SparseCore 0:
  11.4 238.1 all-gather.2
where the time goes:
time: 569 us; the launch traced here: 567 us
  waiting for transfers between devices  223 us (39%)
  matrix products  167 us (29%)
  other arithmetic  72.8 us (13%)
  blocking collectives  52.7 us (9%)
  local copies, waits for them, and re-layouts  20.2 us (4%)
  between operations  15.5 us (3%)
  starting transfers between devices  12.6 us (2%)
    all_gather x1, waiting for transfers between devices, carried_in(): pieces = jax.tree.map(lambda part: lax.all_gather(part, axis), value)  181 us
    dot_general x64, matrix products, compose(): jnp.einsum('phst,pthc->pshc', table.astype(jnp.bfloat16), early_rows, pre...  142 us
    reduce_sum x63, other arithmetic, compose(): jnp.sum(jnp.where(table, early_marks[..., None, :], 0), axis=-1)  57.7 us
    all_gather x1, blocking collectives, carried_in(): pieces = jax.tree.map(lambda part: lax.all_gather(part, axis), value)  52.7 us
    all_to_all x1, waiting for transfers between devices, local(): lax.all_to_all(packed, 'ctx', split_axis=0, concat_axis=0, tiled=True)  25.4 us
    all_to_all x1, waiting for transfers between devices, local(): lax.all_to_all(lax.all_to_all(packed, 'ctx', split_axis=0, concat_axis=0,...  16.5 us
    sub x4, matrix products, local(): expo = jnp.where(allowed, jnp.exp(attention_scores - peak), 0.0)  14.5 us
  transfers between devices with their start and end apart: 3, of which 3 were waited for; matrix products, arithmetic and copies ran while one was open for 6% of the time, Pallas kernels for 0%

commit v1 on v0

--- a/solution.py
+++ b/solution.py
@@ -115,12 +115,20 @@
     ).astype(jnp.bfloat16)
     packed = jnp.dot(placing, sending, preferred_element_type=jnp.float32).astype(jnp.bfloat16)
     packed = packed.reshape(lax.axis_size("ctx"), lax.axis_size("kv"), capacity, heads_dev * width)
-    arrived = lax.all_to_all(
-        lax.all_to_all(packed, "ctx", split_axis=0, concat_axis=0, tiled=True),
-        "kv",
-        split_axis=1,
-        concat_axis=3,
-        tiled=True,
+    arrived = jnp.concatenate(
+        lax.all_to_all(
+            jnp.stack(
+                jnp.split(
+                    lax.all_to_all(packed, "ctx", split_axis=0, concat_axis=0, tiled=True),
+                    lax.axis_size("kv"),
+                    axis=1,
+                )
+            ),
+            "kv",
+            0,
+            0,
+        ),
+        axis=3,
     )
     owner_cache = arrived.reshape(-1, arrived.shape[3])
     return (attention, row_scores, owner_cache)

time: 569 us -> 565 us (level)
  transfers between devices with their start and end apart: 3 -> 3, of which waited for: 3 -> 3; matrix products, arithmetic and copies ran while one was open for 6% -> 7% of each run, Pallas kernels for 0% -> 0%
where the time goes in v1:
time: 565 us; the launch traced here: 563 us
  waiting for transfers between devices  222 us (39%)
  matrix products  166 us (29%)
  other arithmetic  74.3 us (13%)
  blocking collectives  52.7 us (9%)
  local copies, waits for them, and re-layouts  16.7 us (3%)
  between operations  15.5 us (3%)
  starting transfers between devices  12.6 us (2%)
    all_gather x1, waiting for transfers between devices, carried_in(): pieces = jax.tree.map(lambda part: lax.all_gather(part, axis), value)  180 us
    dot_general x64, matrix products, compose(): jnp.einsum('phst,pthc->pshc', table.astype(jnp.bfloat16), early_rows, pre...  141 us
    reduce_sum x63, other arithmetic, compose(): jnp.sum(jnp.where(table, early_marks[..., None, :], 0), axis=-1)  57.6 us
    all_gather x1, blocking collectives, carried_in(): pieces = jax.tree.map(lambda part: lax.all_gather(part, axis), value)  52.7 us
    all_to_all x1, waiting for transfers between devices, local(): lax.all_to_all(packed, 'ctx', split_axis=0, concat_axis=0, tiled=True)  25.3 us
    all_to_all x1, waiting for transfers between devices, local(): lax.all_to_all(jnp.stack(jnp.split(lax.all_to_all(packed, 'ctx', split_ax...  16.5 us
    sub x4, matrix products, local(): expo = jnp.where(allowed, jnp.exp(attention_scores - peak), 0.0)  14.5 us
  transfers between devices with their start and end apart: 3, of which 3 were waited for; matrix products, arithmetic and copies ran while one was open for 7% of the time, Pallas kernels for 0%

profile of v1, /device:TPU:32, one launch (start us, length us, event | category | flops | bytes accessed | tf_op | source)
XLA Modules:
  0.0 562.9 jit_solution(1366251073054927577)
XLA Ops:
  12.2 2.3 copy.55
  16.4 52.7 %all_gather.10 = s32[64,2,2,512]{3,2,1,0:T(2,128)S(1)} all-gather(s32[1,2,2,512]{3,2,1,0:T(2,128)S(1)} %fusion.131), channel_id=1, replica_groups=mesh['ctx'=64,'kv'=4] {'ctx'}, dimensions={0}, use_global_device_ids=true | all-gather | bytes 532480 | tf_op jit(solution)/shard_map/all_gather | solution.py:12
  69.6 180.0 %all-gather.3.cloned.1.call-done = bf16[128,512,2,256]{3,1,2,0:T(8,128)(2,1)} async-done(((bf16[2,512,2,256]{3,1,2,0:T(8,128)(2,1)}), bf16[128,512,2,256]{3,1,2,0:T(8,128)(2,1)}) %all-gather.3.cloned.1.call-update) | async-done | bytes 67108880 | tf_op jit(solution)/shard_map/all_gather | solution.py:12
  249.6 206.5 %while.16 = (s32[]{:T(128)}, s32[2,2,512]{2,1,0:T(2,128)S(1)}, bf16[2,512,2,256]{3,1,2,0:T(8,128)(2,1)S(1)}, s32[]{:T(128)}, s32[64,2,2,512]{3,2,1,0:T(2,128)S(1...) while((s32[]{:T(128)}, s32[2,2,512]{2,1,0:T(2,128)S(1)}, ...), condition=%wide.region_2.3_spmd.clone, body=%wide.region_0.2_spmd.clone.sunk | while | flops 543692800 | bytes 6381168 | solution.py:21
  266.1 2.2 fusion.176
  285.8 2.2 fusion.176
  305.4 2.2 fusion.176
  325.1 2.2 fusion.176
  344.8 2.2 fusion.176
  354.6 2.2 fusion.176
  364.4 2.2 fusion.176
  374.3 2.2 fusion.176
  384.1 2.2 fusion.176
  394.0 2.2 fusion.176
  459.6 3.7 fusion.18
  463.3 8.3 %all-to-all-start = ((bf16[64,4,8,512]{3,2,1,0:T(8,128)(2,1)}), bf16[64,4,8,512]{3,2,1,0:T(8,128)(2,1)S(1)}, u32[]{:S(2)}, u32[]{:S(2)}) async-start(bf16[64,4,8,512]{3,2,1,0:T(8,128)(2,1)} %bitcast.219), calls=%async_computation | async-start | bytes 4194304 | tf_op jit(solution)/shard_map/all_to_all | solution.py:122
  473.1 3.7 fusion.163
  476.8 3.6 fusion.160
  483.2 3.6 fusion.157
  486.9 3.6 fusion.156
  496.7 25.3 %all-to-all-done = bf16[64,4,8,512]{3,2,1,0:T(8,128)(2,1)S(1)} async-done(((bf16[64,4,8,512]{3,2,1,0:T(8,128)(2,1)}), bf16[64,4,8,512]{3,2,1,0:T(8,128)(2,1)S(1)}, u32[]{:S(2)}, u32[]{:S(2)}) %all-to-all-start) | async-done | bytes 2097184 | tf_op jit(solution)/shard_map/all_to_all | solution.py:122
  523.8 4.2 all-to-all-start.1
  532.0 2.3 fusion.79
  537.9 16.5 %all-to-all-done.1 = bf16[4,64,1,8,512]{4,3,1,2,0:T(8,128)(2,1)S(1)} async-done(((bf16[4,64,1,8,512]{4,3,1,2,0:T(8,128)(2,1)}), bf16[4,64,1,8,512]{4,3,1,2,0:T(8,128)(2,1)S(1)}, u32[]{:S(2)}, u32[]{:S(2)}) %all-to-all-start.1) | async-done | bytes 2097184 | tf_op jit(solution)/shard_map/all_to_all | solution.py:119
  (375 shorter events, 212.1 us)
Async XLA Ops:
  7.2 4.2 copy-start.6
  7.2 242.4 %all-gather.3.cloned.1.call-start = ((), (), s32[]{:S(2)}) async-start(), calls=%async_computation.2 | async-start | bytes 68157440 | tf_op jit(solution)/shard_map/all_gather | solution.py:12
  11.8 4.5 copy-start.5
  463.3 58.7 %all-to-all-start = ((bf16[64,4,8,512]{3,2,1,0:T(8,128)(2,1)}), bf16[64,4,8,512]{3,2,1,0:T(8,128)(2,1)S(1)}, u32[]{:S(2)}, u32[]{:S(2)}) async-start(bf16[64,4,8,512]{3,2,1,0:T(8,128)(2,1)} %bitcast.219), calls=%async_computation | async-start | bytes 4194304 | tf_op jit(solution)/shard_map/all_to_all | solution.py:122
  480.5 2.5 copy-start.3
  490.4 2.5 copy-start
  490.4 3.3 copy-start.2
  493.8 1.8 copy-start.4
  523.8 30.7 %all-to-all-start.1 = ((bf16[4,64,1,8,512]{4,3,1,2,0:T(8,128)(2,1)}), bf16[4,64,1,8,512]{4,3,1,2,0:T(8,128)(2,1)S(1)}, u32[]{:S(2)}, u32[]{:S(2)}) async-start(bf16[4,64,1,8,512]{4,3,1,2,0:T(8,128)(2,1)} %pad_maximum_fusion), calls=%async_computation.1 | async-start | bytes 4194304 | tf_op jit(solution)/shard_map/all_to_all | solution.py:119
  532.0 2.5 copy-start.1
Sparse Core Ops, SparseCore 0:
  11.4 238.1 all-gather.2
